TPU v7x, 128 devices: a whole 4x4x4 slice. The times are simulated.
128 devices in a mesh: rows: 32 (over z_hi, x, y), feat: 4 (over z_lo, core).
Axes of the slice: x: 4, y: 4, z: 4 (z_hi: 2, z_lo: 2; z = z_hi * 2 + z_lo), core: 2. Of those that a mesh axis runs over, the one named last changes fastest.
Arguments:
- features: bfloat16 [256, 196608], P('feat', 'rows'), may hold values from -6 to 6
- weight: bfloat16 [256, 256], P('feat'), may hold values from -0.375 to 0.375
- cotangent: bfloat16 [256, 196608], P('feat', 'rows'), may hold values from -6 to 6
- blocks: bfloat16 [32, 256, 128, 128], P('rows', 'feat'), may hold values from -0.25 to 0.25
- row_block: int32 [32, 256], P('rows', 'feat'), may hold values from 0 to 47
- src_owner: int32 [32, 256, 1], P('rows', 'feat'), may hold values from 0 to 31; in each aligned block of 64 rows (0 to 63, 64 to 127, ..., all dimensions but the last counted through in order) at most 4 rows name the same one
- src_block: int32 [32, 256], P('rows', 'feat'), may hold values from 0 to 47
- live: int32 [32, 4], P('rows', 'feat'), may hold values from 8 to 64, as said below
Outputs:
- activation: bfloat16 [256, 196608], P('feat', 'rows')
- feature_grad: bfloat16 [256, 196608], P('feat', 'rows')
- weight_grad: float32 [256, 256], P('feat')
Inputs may be any that keep to these rules, and one draw needn't show every extreme that they name: `src_owner`: among the 64 slots of one device, no owner is named more than 4 times, a bound that some block reaches. Some device has all 64 slots live.
All inputs are finite; a program needn't handle non-finite values.
Results may differ from a plain program's by a relative error of at most 0.024.
Values may be sent and summed in bfloat16 or wider, within the bound.
No kernel may reach another device: no remote copies, remote signals or barrier semaphores. Data moves between devices by JAX's collectives and lax.ppermute only.
A program may use at most 128 MiB of HBM per device.

v0:
```python
import math

import jax
import jax.numpy as jnp
from jax import lax
from jax.sharding import PartitionSpec as P


def plan_slots(owners, row_count, capacity):
    member = (owners[:, None] == jnp.arange(row_count, dtype=jnp.int32)[None, :]).astype(jnp.int32)
    before = jnp.cumsum(member, axis=0) - member
    offset = jnp.sum(before * member, axis=1)
    return owners * capacity + offset


def request_blocks(within, destination, row_count, capacity):
    wanted = (
        jnp.zeros((row_count * capacity,), jnp.int32)
        .at[destination]
        .set(within)
        .reshape(row_count, capacity)
    )
    return lax.all_to_all(wanted, "rows", split_axis=0, concat_axis=0, tiled=True).reshape(
        row_count * capacity
    )


def serve_panels(source, requested, destination, row_count, capacity):
    width, _, block_size = source.shape
    served = jnp.take(source, requested, axis=1).reshape(width, row_count, capacity, block_size)
    arrived = lax.all_to_all(served, "rows", split_axis=1, concat_axis=1, tiled=True).reshape(
        width, row_count * capacity, block_size
    )
    return jnp.take(arrived, destination, axis=1)


def aggregate_slots(picked, tiles, target, local_rows):
    products = jnp.einsum("fsm,snm->fsn", picked, tiles, preferred_element_type=jnp.float32)
    width = products.shape[0]
    block_size = products.shape[2]
    summed = jnp.zeros((width, local_rows, block_size), jnp.float32).at[:, target, :].add(products)
    return summed.reshape(width, local_rows * block_size)


def return_terms(returned, destination, requested, row_count, capacity, local_rows):
    width, _, block_size = returned.shape
    outgoing = (
        jnp.zeros((width, row_count * capacity, block_size), jnp.bfloat16)
        .at[:, destination, :]
        .set(returned)
    )
    outgoing = outgoing.reshape(width, row_count, capacity, block_size)
    incoming = lax.all_to_all(outgoing, "rows", split_axis=1, concat_axis=1, tiled=True).reshape(
        width, row_count * capacity, block_size
    )
    landing = (requested[:, None] == jnp.arange(local_rows, dtype=jnp.int32)[None, :]).astype(
        jnp.bfloat16
    )
    collected = jnp.einsum("fkm,kb->fbm", incoming, landing, preferred_element_type=jnp.float32)
    return collected.reshape(width, local_rows * block_size)


def on_device(features, weight, cotangent, blocks, row_block, src_owner, src_block, live):
    row_count = lax.axis_size("rows")
    feat_count = lax.axis_size("feat")
    quarter, node_count = features.shape
    hidden = quarter * feat_count
    block_size = blocks.shape[2]
    device_slots = blocks.shape[1]
    local_rows = node_count // block_size
    capacity = max(2, 2 * device_slots // row_count)
    living = jnp.arange(device_slots, dtype=jnp.int32) < live[0, 0]
    masked_tiles = blocks[0] * living.astype(jnp.bfloat16)[:, None, None]
    target = row_block[0]
    destination = plan_slots(src_owner[0, :, 0], row_count, capacity)
    requested = request_blocks(src_block[0], destination, row_count, capacity)
    all_features = lax.all_gather(features, "feat", axis=0, tiled=True).reshape(
        hidden, local_rows, block_size
    )
    picked = serve_panels(all_features, requested, destination, row_count, capacity)
    partial_value = aggregate_slots(picked, masked_tiles, target, local_rows)
    aggregated = lax.psum(partial_value, "feat").astype(jnp.bfloat16)
    preact = jnp.dot(weight, aggregated, preferred_element_type=jnp.float32)
    positive = jnp.maximum(preact, 0.0)
    activation = (positive * positive).astype(jnp.bfloat16)
    pre_grad = (2.0 * cotangent.astype(jnp.float32) * positive).astype(jnp.bfloat16)
    nodes_all = node_count * row_count
    weight_part = lax.dot_general(
        pre_grad, aggregated, (((1,), (1,)), ((), ())), preferred_element_type=jnp.float32
    )
    weight_grad = lax.psum(weight_part.astype(jnp.bfloat16), "rows").astype(jnp.float32) * (
        1.0 / math.sqrt(nodes_all)
    )
    grad_part = lax.dot_general(
        weight, pre_grad, (((0,), (0,)), ((), ())), preferred_element_type=jnp.float32
    )
    agg_grad = lax.psum(grad_part, "feat").astype(jnp.bfloat16)
    grad_blocks = agg_grad.reshape(agg_grad.shape[0], local_rows, block_size)
    gathered_rows = jnp.take(grad_blocks, target, axis=1)
    returned = jnp.einsum(
        "fsn,snm->fsm", gathered_rows, masked_tiles, preferred_element_type=jnp.float32
    ).astype(jnp.bfloat16)
    collected = return_terms(returned, destination, requested, row_count, capacity, local_rows)
    feature_grad = lax.psum_scatter(collected, "feat", scatter_dimension=0, tiled=True).astype(
        jnp.bfloat16
    )
    return (activation, feature_grad, weight_grad)


def solution(mesh):
    placed = (
        P("feat", "rows"),
        P("feat", None),
        P("feat", "rows"),
        P("rows", "feat", None, None),
        P("rows", "feat"),
        P("rows", "feat", None),
        P("rows", "feat"),
        P("rows", "feat"),
    )
    return jax.shard_map(
        on_device,
        mesh=mesh,
        in_specs=placed,
        out_specs=(P("feat", "rows"), P("feat", "rows"), P("feat", None)),
        check_vma=False,
    )
```

profile of v0, /device:TPU:0, one launch (start us, length us, event | category | flops | bytes accessed | tf_op | source)
XLA Modules:
  0.0 877.0 jit_solution(15350954676580061722)
XLA Ops:
  7.2 0.7 all-gather.2.cloned.1.call-update
  7.9 0.7 fusion.21
  8.6 0.1 reduce_window_sum.11
  8.7 0.8 select_reduce_fusion
  9.6 0.7 fusion.27
  10.3 0.9 scatter_custom_fusion
  11.2 0.1 all_to_all.12
  11.3 20.3 %all_to_all.19 = s32[32,1,4]{2,1,0:T(1,128)S(1)} all-to-all(s32[32,1,4]{2,1,0:T(1,128)S(1)} %bitcast.78), channel_id=1, replica_groups=mesh['rows'=32,'feat'=4] {'rows'}, dimensions={0} | all-to-all | bytes 1024 | tf_op jit(solution)/shard_map/all_to_all | solution.py:23
  31.6 0.5 broadcast.152
  32.1 0.7 reduce.5
  32.8 0.1 reshape.157
  32.9 0.1 copy.33
  33.0 0.1 copy.34
  33.1 16.8 %all-gather.2.cloned.1.call-done = bf16[256,6144]{1,0:T(8,128)(2,1)} async-done(((bf16[64,6144]{1,0:T(8,128)(2,1)}), bf16[256,6144]{1,0:T(8,128)(2,1)}) %all-gather.2.cloned.1.call-update) | async-done | bytes 3145744 | tf_op jit(solution)/shard_map/all_gather | solution.py:77
  49.9 4.7 copy.35
  54.6 3.5 copy.36
  58.1 6.5 gather_fusion
  64.5 7.4 broadcast_select_fusion
  72.0 9.5 %all-to-all-start.1 = ((bf16[256,32,4,128]{3,0,2,1:T(8,128)(2,1)}), bf16[256,32,4,128]{3,0,2,1:T(8,128)(2,1)}, u32[]{:S(2)}, u32[]{:S(2)}) async-start(bf16[256,32,4,128]{3,0,2,1:T(8,128)(2,1)} %broadcast_select_fusion), calls=%async_computation.1 | async-start | bytes 16777216 | tf_op jit(solution)/shard_map/all_to_all | solution.py:31
  82.2 122.9 %all-to-all-done.1 = bf16[256,32,4,128]{3,0,2,1:T(8,128)(2,1)} async-done(((bf16[256,32,4,128]{3,0,2,1:T(8,128)(2,1)}), bf16[256,32,4,128]{3,0,2,1:T(8,128)(2,1)}, u32[]{:S(2)}, u32[]{:S(2)}) %all-to-all-start.1) | async-done | bytes 8388640 | tf_op jit(solution)/shard_map/all_to_all | solution.py:31
  205.1 6.6 gather_fusion.1
  211.7 6.7 fusion.3
  218.5 3.5 broadcast_in_dim.47
  221.9 19.3 %scatter_fusion = f32[256,48,128]{2,0,1:T(8,128)} fusion(f32[256,48,128]{2,0,1:T(8,128)} %broadcast_in_dim.47, s32[64]{0:T(128)S(1)} %fusion.26, f32[64,256,128]{2,1,0:T(8,128)} %fusion.3), kind=kCustom, calls=%fused_computation.4 | custom fusion | flops 2097152 | bytes 25166080 | tf_op jit(solution)/shard_map/scatter-add | solution.py:41
  241.3 6.6 copy.37
  247.9 111.1 %all-reduce.2 = bf16[256,6144]{0,1:T(8,128)(2,1)S(1)} all-reduce(f32[256,6144]{0,1:T(8,128)} %bitcast.74), channel_id=1, replica_groups=mesh['rows'=32,'feat'=4] {'feat'}, use_global_device_ids=true, to_apply=%region_4.5 | all-reduce | flops 1572864 | bytes 9437184 | tf_op jit(solution)/shard_map/psum | solution.py:82
  359.0 2.0 multiply_convert_fusion.1
  361.0 1.2 copy-done.2
  362.1 3.7 convolution_bitcast_fusion
  365.9 112.9 %all-reduce.3 = bf16[256,6144]{0,1:T(8,128)(2,1)} all-reduce(f32[256,6144]{0,1:T(8,128)} %convolution_bitcast_fusion), channel_id=1, replica_groups=mesh['rows'=32,'feat'=4] {'feat'}, use_global_device_ids=true, to_apply=%region_5.6 | all-reduce | flops 1572864 | bytes 9437184 | tf_op jit(solution)/shard_map/psum | solution.py:97
  478.7 4.6 copy.38
  483.4 4.9 gather_fusion.2
  488.3 7.0 convert_bitcast_fusion
  495.2 6.3 copy.40
  501.6 5.3 broadcast_in_dim.55
  506.9 12.0 %scatter_fusion.1 = bf16[256,128,128]{2,0,1:T(8,128)(2,1)} fusion(bf16[256,128,128]{2,0,1:T(8,128)(2,1)} %broadcast_in_dim.55, s32[64]{0:T(128)S(1)} %fusion.27, bf16[64,256,128]{2,1,0:T(8,128)(2,1)} %copy.40), kind=kCustom, calls=%fused_computation.5 | custom fusion | bytes 12583168 | tf_op jit(solution)/shard_map/scatter | solution.py:50
  518.9 11.0 %copy.41 = bf16[256,32,4,128]{3,2,0,1:T(4,128)(2,1)} copy(bf16[256,32,4,128]{3,0,2,1:T(8,128)(2,1)} %bitcast.69) | data formatting | bytes 16777216 | tf_op jit(solution)/shard_map/reshape | solution.py:52
  529.9 17.5 %all-to-all-start.2 = ((bf16[256,32,4,128]{3,2,0,1:T(4,128)(2,1)}), bf16[256,32,4,128]{3,2,0,1:T(4,128)(2,1)}, u32[]{:S(2)}, u32[]{:S(2)}) async-start(bf16[256,32,4,128]{3,2,0,1:T(4,128)(2,1)} %copy.41), calls=%async_computation.2 | async-start | bytes 16777216 | tf_op jit(solution)/shard_map/all_to_all | solution.py:53
  547.5 0.0 reduce-scatter.2.cloned.1.call-start
  547.5 0.1 reshape.160
  547.6 119.3 %all-to-all-done.2 = bf16[256,32,4,128]{3,2,0,1:T(4,128)(2,1)} async-done(((bf16[256,32,4,128]{3,2,0,1:T(4,128)(2,1)}), bf16[256,32,4,128]{3,2,0,1:T(4,128)(2,1)}, u32[]{:S(2)}, u32[]{:S(2)}) %all-to-all-start.2) | async-done | bytes 8388640 | tf_op jit(solution)/shard_map/all_to_all | solution.py:53
  666.9 6.1 copy.42
  673.0 1.2 fusion.23
  674.2 5.3 copy.46
  679.5 2.2 fusion.16
  681.7 185.4 %psum.23 = bf16[64,256]{1,0:T(8,128)(2,1)S(1)} all-reduce(bf16[64,256]{1,0:T(8,128)(2,1)S(1)} %fusion.16), channel_id=1, replica_groups=mesh['rows'=32,'feat'=4] {'rows'}, use_global_device_ids=true, to_apply=%region_8.9 | all-reduce | flops 16384 | bytes 65536 | tf_op jit(solution)/shard_map/psum | solution.py:91
  867.1 0.6 convert_multiply_fusion
  867.8 2.4 convert_element_type.50
  (24 shorter events, 0.1 us)
Async XLA Ops:
  7.2 351.9 %copy-start = (bf16[64,256]{1,0:T(8,128)(2,1)S(1)}, bf16[64,256]{1,0:T(8,128)(2,1)}, u32[]{:S(2)}) copy-start(bf16[64,256]{1,0:T(8,128)(2,1)} %param.9) | copy-start | bytes 98308
  7.2 42.7 %all-gather.2.cloned.1.call-start = ((), (), s32[]{:S(2)}) async-start(), calls=%async_computation.4 | async-start | bytes 3932160 | tf_op jit(solution)/shard_map/all_gather | solution.py:77
  72.0 10.2 %copy-start.6 = (s32[1,64]{1,0:T(1,128)S(1)}, s32[1,64]{1,0:T(1,128)}, u32[]{:S(2)}) copy-start(s32[1,64]{1,0:T(1,128)} %param.12) | copy-start | bytes 772
  72.0 10.3 %copy-start.5 = (s32[1,64,1]{1,2,0:T(1,128)S(1)}, s32[1,64,1]{1,2,0:T(1,128)}, u32[]{:S(2)}) copy-start(s32[1,64,1]{1,2,0:T(1,128)} %param.13) | copy-start | bytes 772
  72.0 133.2 %all-to-all-start.1 = ((bf16[256,32,4,128]{3,0,2,1:T(8,128)(2,1)}), bf16[256,32,4,128]{3,0,2,1:T(8,128)(2,1)}, u32[]{:S(2)}, u32[]{:S(2)}) async-start(bf16[256,32,4,128]{3,0,2,1:T(8,128)(2,1)} %broadcast_select_fusion), calls=%async_computation.1 | async-start | bytes 16777216 | tf_op jit(solution)/shard_map/all_to_all | solution.py:31
  205.1 6.6 copy-start.3
  359.0 3.1 copy-start.4
  361.0 1.2 copy-start.2
  529.9 137.0 %all-to-all-start.2 = ((bf16[256,32,4,128]{3,2,0,1:T(4,128)(2,1)}), bf16[256,32,4,128]{3,2,0,1:T(4,128)(2,1)}, u32[]{:S(2)}, u32[]{:S(2)}) async-start(bf16[256,32,4,128]{3,2,0,1:T(4,128)(2,1)} %copy.41), calls=%async_computation.2 | async-start | bytes 16777216 | tf_op jit(solution)/shard_map/all_to_all | solution.py:53
  547.5 320.3 %reduce-scatter.2.cloned.1.call-start = ((), (), s32[]{:S(2)}) async-start(), calls=%async_computation.5 | async-start | bytes 7864320 | tf_op jit(solution)/shard_map/reduce_scatter | solution.py:104
  679.5 190.6 %copy-start.1 = (bf16[64,256]{1,0:T(8,128)(2,1)S(1)}, bf16[64,256]{1,0:T(8,128)(2,1)}, u32[]{:S(2)}) copy-start(bf16[64,256]{1,0:T(8,128)(2,1)} %param.9) | copy-start | bytes 98308
Sparse Core Ops, SparseCore 0:
  9.7 40.1 all-gather.1
  679.6 73.4 reduce-scatter.1
where the time goes:
time: 878 us; the launch traced here: 877 us
  blocking collectives  430 us (49%)
  waiting for transfers between devices  260 us (30%)
  local copies, waits for them, and re-layouts  90 us (10%)
  other arithmetic  32.8 us (4%)
  starting transfers between devices  27.2 us (3%)
  matrix products  22.8 us (3%)
  between operations  14.9 us (2%)
    psum x1, blocking collectives, on_device(): lax.psum(weight_part.astype(jnp.bfloat16), 'rows').astype(jnp.float32)  185 us
    all_to_all x1, waiting for transfers between devices, serve_panels(): lax.all_to_all(served, 'rows', split_axis=1, concat_axis=1, tiled=True)  123 us
    all_to_all x1, waiting for transfers between devices, return_terms(): lax.all_to_all(outgoing, 'rows', split_axis=1, concat_axis=1, tiled=True)  119 us
    psum x1, blocking collectives, on_device(): agg_grad = lax.psum(grad_part, 'feat').astype(jnp.bfloat16)  113 us
    psum x1, blocking collectives, on_device(): aggregated = lax.psum(partial_value, 'feat').astype(jnp.bfloat16)  111 us
    all_to_all x1, blocking collectives, request_blocks(): lax.all_to_all(wanted, 'rows', split_axis=0, concat_axis=0, tiled=True)  20.3 us
    scatter-add x1, other arithmetic, aggregate_slots(): jnp.zeros((width, local_rows, block_size), jnp.float32).at[:, target, :]  19.3 us
  transfers between devices with their start and end apart: 4, of which 3 were waited for; matrix products, arithmetic and copies ran while one was open for 1% of the time, Pallas kernels for 0%

commit v1 on v0

v1 whole, which is shorter than its diff:
```python
import functools
import math

import jax
import jax.numpy as jnp
from jax import lax
from jax.experimental import pallas as pl
from jax.experimental.pallas import tpu as pltpu
from jax.sharding import PartitionSpec as P

BF = jnp.bfloat16
F32 = jnp.float32
I32 = jnp.int32
VMEM_LIMIT = 56 * 1024 * 1024
GROUP = 8


def params():
    return pltpu.CompilerParams(vmem_limit_bytes=VMEM_LIMIT)


def core_swap(x):
    return lax.ppermute(x, "feat", [(0, 1), (1, 0), (2, 3), (3, 2)])


def chip_swap(x):
    return lax.ppermute(x, "feat", [(0, 2), (2, 0), (1, 3), (3, 1)])


def gather_feat(x):
    far = chip_swap(x)
    return (x, core_swap(x), far, core_swap(far))


def relative(x, axis, me):
    a = jnp.split(x, 4, axis=axis)
    low = (me & 1) == 1
    high = (me & 2) == 2
    b = [jnp.where(low, a[i ^ 1], a[i]) for i in range(4)]
    c = [jnp.where(high, b[i ^ 2], b[i]) for i in range(4)]
    return jnp.concatenate(c, axis=axis)


def exact_dot(a, b):
    return jnp.dot(a.astype(BF), b.astype(BF), preferred_element_type=F32)


def ranks(want):
    n = want.shape[-1]
    upper = jnp.arange(n)[:, None] < jnp.arange(n)[None, :]
    return exact_dot(want, upper).astype(I32)


def serve_kernel(capacity, index, features, out):
    row = pl.program_id(0)
    width = features.shape[0]
    for k in range(capacity):
        start = pl.multiple_of(index[row * capacity + k] * 128, 128)
        out[0, k * width : (k + 1) * width, :] = features[:, pl.ds(start, 128)]


def serve(features, index, rows, capacity):
    width, nodes = features.shape
    return pl.pallas_call(
        functools.partial(serve_kernel, capacity),
        grid_spec=pltpu.PrefetchScalarGridSpec(
            num_scalar_prefetch=1,
            grid=(rows,),
            in_specs=[pl.BlockSpec((width, nodes), lambda r, i: (0, 0))],
            out_specs=pl.BlockSpec((1, capacity * width, 128), lambda r, i: (r, 0, 0)),
        ),
        out_shape=jax.ShapeDtypeStruct((rows, capacity * width, 128), BF),
        compiler_params=params(),
        cost_estimate=pl.CostEstimate(
            flops=0, bytes_accessed=rows * capacity * width * 256, transcendentals=0
        ),
    )(index, features)


def aggregate_kernel(lists, slots, source, target, live, panels, *refs):
    tiles = refs[:lists]
    out, held, panel, acc, sems = refs[lists:]
    blocks = out.shape[0]
    copies = [pltpu.make_async_copy(panels, panel, sems.at[lists])]
    copies += [pltpu.make_async_copy(tiles[j], held.at[j], sems.at[j]) for j in range(lists)]
    for c in copies:
        c.start()
    acc[...] = jnp.zeros_like(acc)
    copies[0].wait()
    for j in range(lists):
        copies[j + 1].wait()

        def body(g, carry, j=j):
            base = g * GROUP
            products = []
            for u in range(GROUP):
                s = j * slots + base + u
                products.append(
                    lax.dot_general(
                        panel[source[s]],
                        held[j, base + u],
                        (((1,), (1,)), ((), ())),
                        preferred_element_type=F32,
                    )
                )
            for u in range(GROUP):
                t = target[j * slots + base + u]
                acc[t] = acc[t] + products[u]
            return carry

        lax.fori_loop(0, (live[j] + GROUP - 1) // GROUP, body, 0)
    out[...] = acc[:blocks].astype(BF)


def aggregate(panels, tiles, source, target, live, blocks):
    lists = len(tiles)
    slots, size, _ = tiles[0].shape
    entries, width, _ = panels.shape
    any_spec = pl.BlockSpec(memory_space=pl.ANY)
    return pl.pallas_call(
        functools.partial(aggregate_kernel, lists, slots),
        grid_spec=pltpu.PrefetchScalarGridSpec(
            num_scalar_prefetch=3,
            grid=(1,),
            in_specs=[any_spec] * (lists + 1),
            out_specs=pl.BlockSpec((blocks, width, size), lambda i, *_: (0, 0, 0)),
            scratch_shapes=[
                pltpu.VMEM((lists, slots, size, size), BF),
                pltpu.VMEM((entries, width, size), BF),
                pltpu.VMEM((blocks + 1, width, size), F32),
                pltpu.SemaphoreType.DMA((lists + 1,)),
            ],
        ),
        out_shape=jax.ShapeDtypeStruct((blocks, width, size), BF),
        compiler_params=params(),
        cost_estimate=pl.CostEstimate(
            flops=2 * lists * slots * width * size * size,
            bytes_accessed=entries * width * size * 2 + lists * slots * size * size * 2,
            transcendentals=0,
        ),
    )(source, target, live, panels, *tiles)


def middle_kernel(step, weight, a0, a1, a2, a3, c0, c1, c2, c3, act, grad, wgrad):
    width = a0.shape[1]
    x = jnp.concatenate(
        [jnp.concatenate([a[b] for b in range(step)], axis=1) for a in (a0, a1, a2, a3)], axis=0
    )
    w = weight[...]
    preact = jnp.dot(w, x, preferred_element_type=F32)
    positive = jnp.maximum(preact, 0.0)
    own = positive[:width]
    act[...] = (own * own).astype(BF)
    cot = jnp.concatenate([c[...] for c in (c0, c1, c2, c3)], axis=0)
    pre = (2.0 * cot.astype(F32) * positive).astype(BF)
    g = lax.dot_general(
        w[:, :width], pre, (((0,), (0,)), ((), ())), preferred_element_type=F32
    ).astype(BF)
    for b in range(step):
        grad[b] = g[:, b * 128 : (b + 1) * 128]
    part = lax.dot_general(
        pre[:width], x, (((1,), (1,)), ((), ())), preferred_element_type=F32
    )

    @pl.when(pl.program_id(0) == 0)
    def _():
        wgrad[...] = part

    @pl.when(pl.program_id(0) > 0)
    def _():
        wgrad[...] = wgrad[...] + part


def middle(weight, aggregated, cotangent):
    blocks, width, size = aggregated[0].shape
    hidden = weight.shape[0]
    step = 8 if blocks % 8 == 0 else 1
    a_spec = pl.BlockSpec((step, width, size), lambda i: (i, 0, 0))
    c_spec = pl.BlockSpec((width, step * size), lambda i: (0, i))
    w_spec = pl.BlockSpec((width, hidden), lambda i: (0, 0))
    return pl.pallas_call(
        functools.partial(middle_kernel, step),
        grid=(blocks // step,),
        in_specs=[pl.BlockSpec((hidden, hidden), lambda i: (0, 0))] + [a_spec] * 4 + [c_spec] * 4,
        out_specs=[c_spec, a_spec, w_spec],
        out_shape=[
            jax.ShapeDtypeStruct((width, blocks * size), BF),
            jax.ShapeDtypeStruct((blocks, width, size), BF),
            jax.ShapeDtypeStruct((width, hidden), F32),
        ],
        compiler_params=params(),
        cost_estimate=pl.CostEstimate(
            flops=2 * hidden * (hidden + 2 * width) * blocks * size,
            bytes_accessed=10 * blocks * width * size * 2,
            transcendentals=0,
        ),
    )(weight, *aggregated, *cotangent)


def terms_kernel(lists, slots, dest, target, again, live, grads, *refs):
    tiles = refs[:lists]
    out, held, made, sems = refs[lists:]
    entries = out.shape[0]
    copies = [pltpu.make_async_copy(tiles[j], held.at[j], sems.at[j]) for j in range(lists)]
    for c in copies:
        c.start()
    for j in range(lists):
        copies[j].wait()

        def body(g, carry, j=j):
            base = g * GROUP
            products = []
            for u in range(GROUP):
                s = j * slots + base + u
                products.append(
                    jnp.dot(grads[target[s]], held[j, base + u], preferred_element_type=F32)
                )
            for u in range(GROUP):
                s = j * slots + base + u
                d = dest[s]
                kept = jnp.where(again[s] > 0, made[d].astype(F32), 0.0)
                made[d] = (kept + products[u]).astype(BF)
            return carry

        lax.fori_loop(0, (live[j] + GROUP - 1) // GROUP, body, 0)
    last = pltpu.make_async_copy(made.at[pl.ds(0, entries)], out, sems.at[lists])
    last.start()
    last.wait()


def terms(grads, tiles, dest, target, again, live, entries):
    lists = len(tiles)
    slots, size, _ = tiles[0].shape
    blocks, width, _ = grads.shape
    any_spec = pl.BlockSpec(memory_space=pl.ANY)
    return pl.pallas_call(
        functools.partial(terms_kernel, lists, slots),
        grid_spec=pltpu.PrefetchScalarGridSpec(
            num_scalar_prefetch=4,
            grid=(1,),
            in_specs=[pl.BlockSpec((blocks, width, size), lambda i, *_: (0, 0, 0))]
            + [any_spec] * lists,
            out_specs=any_spec,
            scratch_shapes=[
                pltpu.VMEM((lists, slots, size, size), BF),
                pltpu.VMEM((entries + 1, width, size), BF),
                pltpu.SemaphoreType.DMA((lists + 1,)),
            ],
        ),
        out_shape=jax.ShapeDtypeStruct((entries, width, size), BF),
        compiler_params=params(),
        cost_estimate=pl.CostEstimate(
            flops=2 * lists * slots * width * size * size,
            bytes_accessed=entries * width * size * 2 + lists * slots * size * size * 2,
            transcendentals=0,
        ),
    )(dest, target, again, live, grads, *tiles)


def collect_kernel(capacity, blocks, index, count, incoming, out, acc):
    row = pl.program_id(0)
    width = out.shape[0]

    @pl.when(row == 0)
    def _():
        acc[...] = jnp.zeros_like(acc)

    def body(g, carry):
        for u in range(4):
            k = g * 4 + u
            t = index[row * capacity + k]
            start = pl.multiple_of(k * width, width)
            acc[t] = acc[t] + incoming[0, pl.ds(start, width), :].astype(F32)
        return carry

    lax.fori_loop(0, (count[row] + 3) // 4, body, 0)

    @pl.when(row == pl.num_programs(0) - 1)
    def _():
        for b in range(blocks):
            out[:, b * 128 : (b + 1) * 128] = acc[b].astype(BF)


def collect(incoming, index, count, blocks, width, capacity):
    rows = incoming.shape[0]
    return pl.pallas_call(
        functools.partial(collect_kernel, capacity, blocks),
        grid_spec=pltpu.PrefetchScalarGridSpec(
            num_scalar_prefetch=2,
            grid=(rows,),
            in_specs=[pl.BlockSpec((1, capacity * width, 128), lambda r, *_: (r, 0, 0))],
            out_specs=pl.BlockSpec((width, blocks * 128), lambda r, *_: (0, 0)),
            scratch_shapes=[pltpu.VMEM((blocks + 1, width, 128), F32)],
        ),
        out_shape=jax.ShapeDtypeStruct((width, blocks * 128), BF),
        compiler_params=params(),
        cost_estimate=pl.CostEstimate(
            flops=rows * capacity * width * 128,
            bytes_accessed=rows * capacity * width * 256,
            transcendentals=0,
        ),
    )(index, count, incoming)


def exchange(x):
    return lax.all_to_all(x, "rows", split_axis=0, concat_axis=0, tiled=True)


def on_device(features, weight, cotangent, blocks, row_block, src_owner, src_block, live):
    rows = lax.axis_size("rows")
    feats = lax.axis_size("feat")
    me = lax.axis_index("feat")
    width, nodes = features.shape
    size = blocks.shape[2]
    slots = blocks.shape[1]
    local = nodes // size
    capacity = max(2, 2 * slots // rows) * feats

    tiles = gather_feat(blocks[0])

    here = jnp.arange(slots, dtype=I32)
    alive = here < live[0, 0]
    code = jnp.where(alive, src_owner[0, :, 0] * 64 + src_block[0], -1)
    goal = jnp.where(alive, row_block[0], local)
    note = gather_feat(jnp.stack([code, goal]))
    code = jnp.concatenate([n[0] for n in note])
    target = jnp.concatenate([n[1] for n in note])
    valid = code >= 0
    counts = jnp.stack([jnp.sum((n[0] >= 0).astype(I32)) for n in note])
    owner = jnp.where(valid, code >> 6, -1)
    block = jnp.where(valid, code & 63, -1)
    owner_hot = owner[:, None] == jnp.arange(rows, dtype=I32)[None, :]
    block_hot = block[:, None] == jnp.arange(local, dtype=I32)[None, :]
    want = exact_dot(owner_hot.T, block_hot) > 0.5
    rank = ranks(want)
    request = jnp.pad(want.astype(I32), ((0, 0), (0, 128 - local)))
    asked = exchange(request)[:, :local]
    asked_rank = ranks(asked)
    asked_count = jnp.sum(asked, axis=1)
    at = jnp.arange(capacity, dtype=I32)[None, :, None]
    chosen = (asked[:, None, :] > 0) & (asked_rank[:, None, :] == at)
    index = jnp.sum(jnp.where(chosen, jnp.arange(local, dtype=I32), 0), axis=2)
    index_flat = index.reshape(-1)
    index_sum = jnp.where(
        jnp.arange(capacity, dtype=I32)[None, :] < asked_count[:, None], index, local
    ).reshape(-1)

    slot_rank = jnp.sum(jnp.where(block_hot, exact_dot(owner_hot, rank), 0.0), axis=1).astype(I32)
    place = owner * capacity + slot_rank
    source = jnp.where(valid, place, 0)
    dest = jnp.where(valid, place, rows * capacity)
    order = jnp.arange(feats * slots, dtype=I32)
    again = jnp.any(
        (code[:, None] == code[None, :]) & (order[None, :] < order[:, None]), axis=1
    ).astype(I32)

    weights = relative(jnp.concatenate(gather_feat(weight), axis=0), 1, me)
    cotangents = gather_feat(cotangent)

    served = serve(features, index_flat, rows, capacity)
    panels = exchange(served).reshape(rows * capacity, width, size)
    own = aggregate(panels, tiles, source, target, counts, local)
    aggregated = gather_feat(own)
    activation, grads, weight_part = middle(weights, aggregated, cotangents)
    made = terms(grads, tiles, dest, target, again, counts, rows * capacity)
    returned = exchange(made.reshape(rows, capacity * width, size))

    total = relative(weight_part, 1, me)
    step = 1
    while step < rows:
        total = total + lax.ppermute(total, "rows", [(i, i ^ step) for i in range(rows)])
        step *= 2
    weight_grad = total * (1.0 / math.sqrt(nodes * rows))
    feature_grad = collect(returned, index_sum, asked_count, local, width, capacity)
    return (activation, feature_grad, weight_grad)


def solution(mesh):
    placed = (
        P("feat", "rows"),
        P("feat", None),
        P("feat", "rows"),
        P("rows", "feat", None, None),
        P("rows", "feat"),
        P("rows", "feat", None),
        P("rows", "feat"),
        P("rows", "feat"),
    )
    return jax.shard_map(
        on_device,
        mesh=mesh,
        in_specs=placed,
        out_specs=(P("feat", "rows"), P("feat", "rows"), P("feat", None)),
        check_vma=False,
    )
```

time: 878 us -> 422 us (0.48)
  blocking collectives: 430 us -> 20.3 us
  local copies, waits for them, and re-layouts: 90 us -> 3.11 us
  Pallas kernels: 0 us -> 60.8 us
  starting transfers between devices: 27.2 us -> 62.5 us
  matrix products: 22.8 us -> 0.72 us
  other arithmetic: 32.8 us -> 12.6 us
  between operations: 14.9 us -> 1.51 us
    psum x3 -> x0, blocking collectives: 409 us -> none  [the longest x1 185 us: on_device(): lax.psum(weight_part.astype(jnp.bfloat16), 'rows').astype(jnp.float32)]
    ppermute x0 -> x20, waiting for transfers between devices: none -> 258 us  [the longest x5 152 us: chip_swap(): return lax.ppermute(x, 'feat', [(0, 2), (2, 0), (1, 3), (3, 1)])]
    all_to_all x2, waiting for transfers between devices: 242 us -> 0.01 us  [exchange(): return lax.all_to_all(x, 'rows', split_axis=0, concat_axis=0, tiled=True)]
    pallas_call x0 -> x5, Pallas kernels: none -> 60.8 us  [the longest x1 18.1 us: collect(): pl.pallas_call(functools.partial(collect_kernel, capacity, blocks), grid_...]
    ppermute x0 -> x20, starting transfers between devices: none -> 44.3 us  [the longest x5 36.5 us: on_device(): lax.ppermute(total, 'rows', [(i, i ^ step) for i in range(rows)])]
    dot_general x6 -> x3, matrix products: 22.8 us -> 0.72 us  [exact_dot(): return jnp.dot(a.astype(BF), b.astype(BF), preferred_element_type=F32)]
    scatter-add x1 -> x0, other arithmetic: 19.3 us -> none  [aggregate_slots(): jnp.zeros((width, local_rows, block_size), jnp.float32).at[:, target, :]]
    reshape x5 -> x1, local copies, waits for them, and re-layouts: 19.4 us -> 0.66 us  [on_device(): index_flat = index.reshape(-1)]
  transfers between devices with their start and end apart: 4 -> 22, of which waited for: 3 -> 10; matrix products, arithmetic and copies ran while one was open for 1% -> 3% of each run, Pallas kernels for 0% -> 2%
where the time goes in v1:
time: 422 us; the launch traced here: 420 us
  waiting for transfers between devices  258 us (61%)
  starting transfers between devices  62.5 us (15%)
  Pallas kernels  60.8 us (14%)
  blocking collectives  20.3 us (5%)
  other arithmetic  12.6 us (3%)
    ppermute x5, waiting for transfers between devices, chip_swap(): return lax.ppermute(x, 'feat', [(0, 2), (2, 0), (1, 3), (3, 1)])  152 us
    ppermute x5, waiting for transfers between devices, on_device(): lax.ppermute(total, 'rows', [(i, i ^ step) for i in range(rows)])  104 us
    ppermute x5, starting transfers between devices, on_device(): lax.ppermute(total, 'rows', [(i, i ^ step) for i in range(rows)])  36.5 us
    all_to_all x1, blocking collectives, exchange(): return lax.all_to_all(x, 'rows', split_axis=0, concat_axis=0, tiled=True)  20.3 us
    all_to_all x2, starting transfers between devices, exchange(): return lax.all_to_all(x, 'rows', split_axis=0, concat_axis=0, tiled=True)  18.2 us
    pallas_call x1, Pallas kernels, collect(): pl.pallas_call(functools.partial(collect_kernel, capacity, blocks), grid_...  18.1 us
    pallas_call x1, Pallas kernels, serve(): pl.pallas_call(functools.partial(serve_kernel, capacity), grid_spec=pltpu...  14.4 us
    pallas_call x1, Pallas kernels, aggregate(): pl.pallas_call(functools.partial(aggregate_kernel, lists, slots), grid_sp...  10.1 us
  transfers between devices with their start and end apart: 22, of which 10 were waited for; matrix products, arithmetic and copies ran while one was open for 3% of the time, Pallas kernels for 2%

profile of v1, /device:TPU:0, one launch (start us, length us, event | category | flops | bytes accessed | tf_op | source)
XLA Modules:
  0.0 419.8 jit_solution(15477005411915256106)
XLA Ops:
  1.3 0.7 compare_select_fusion
  2.0 2.1 collective-permute-start.4
  4.1 1.3 fusion.10
  5.6 0.3 collective-permute-start.5
  5.9 0.9 collective-permute-done.5
  6.9 0.3 convolution_compare_fusion
  7.1 20.3 %all_to_all.27 = s32[32,1,128]{2,1,0:T(1,128)S(1)} all-to-all(s32[32,1,128]{2,1,0:T(1,128)S(1)} %bitcast.56), channel_id=1, replica_groups=mesh['rows'=32,'feat'=4] {'rows'}, dimensions={0} | all-to-all | bytes 32768 | tf_op jit(solution)/shard_map/all_to_all | solution.py:306
  27.6 0.6 select_reduce_fusion
  28.2 0.7 reshape.160.index
  28.8 14.4 %shard_map.103 = bf16[32,1024,128]{2,1,0:T(8,128)(2,1)} custom-call(s32[512]{0:T(512)} %reshape.160.index, bf16[64,6144]{1,0:T(8,128)(2,1)} %features.1), custom_call_target="tpu_custom_call" | custom-call | bytes 8388608 | tf_op jit(solution)/shard_map/pallas_call | solution.py:64
  43.2 5.2 %all-to-all-start.1 = ((bf16[32,1024,128]{2,1,0:T(8,128)(2,1)}), bf16[32,1024,128]{2,1,0:T(8,128)(2,1)}, u32[]{:S(2)}, u32[]{:S(2)}) async-start(bf16[32,1024,128]{2,1,0:T(8,128)(2,1)} %shard_map.103), calls=%async_computation.1 | async-start | bytes 16777216 | tf_op jit(solution)/shard_map/all_to_all | solution.py:306
  48.5 1.1 collective-permute-start.7
  49.6 134.6 %collective-permute-done.7.refs_2_ = bf16[64,128,128]{2,1,0:T(8,128)(2,1)} collective-permute-done((bf16[64,128,128]{2,1,0:T(8,128)(2,1)S(1)}, bf16[64,128,128]{2,1,0:T(8,128)(2,1)}, u32[]{:S(2)}, u32[]{:S(2)}) %collective-permute-start.7) | collective-permute-done | bytes 2097184 | tf_op jit(solution)/shard_map/ppermute | solution.py:27
  184.2 1.0 collective-permute-start.13
  185.2 0.6 fusion.12
  185.9 0.7 fusion.11
  186.6 0.6 fusion.13
  187.2 3.2 pad_add_fusion.3.live
  190.4 0.7 pad_add_fusion.2.target
  191.1 0.3 fusion
  191.4 0.6 broadcast_select_fusion.13
  192.1 10.1 %shard_map.104.a0 = bf16[48,64,128]{2,1,0:T(8,128)(2,1)} custom-call(s32[256]{0:T(256)} %get-tuple-element.22.source, s32[256]{0:T(256)} %pad_add_fusion.2.target, s32[4]{0:T(128)} %pad_add_fusion.3.live, bf16[512,64,128]{2,1,0:T(8,128)(2,1)} %bitcast.18.panels, bf16[64,128,128]{2,1,0:T(8,128)(2,1)} %bitcast.49, ...), custom_call_target="tpu_custom_call" | custom-call | flops 536870912 | bytes 16777216 | tf_op jit(solution)/shard_map/pallas_call | solution.py:120
  202.2 1.1 collective-permute-start.10
  203.5 0.8 collective-permute-start.1
  204.5 0.3 collective-permute-start.14
  205.1 17.5 %collective-permute-done.10.a2 = bf16[48,64,128]{2,1,0:T(8,128)(2,1)S(1)} collective-permute-done((bf16[48,64,128]{2,1,0:T(8,128)(2,1)}, bf16[48,64,128]{2,1,0:T(8,128)(2,1)S(1)}, u32[]{:S(2)}, u32[]{:S(2)}) %collective-permute-start.10) | collective-permute-done | bytes 786464 | tf_op jit(solution)/shard_map/ppermute | solution.py:27
  222.7 0.6 convert_element_type.46.again
  223.3 0.5 collective-permute-start.2
  223.8 1.1 collective-permute-done.2
  225.0 0.8 pad_maximum_fusion.weight
  225.8 0.9 copy-done.3
  226.7 0.3 copy-done.4
  227.2 0.9 copy-done.6
  228.1 8.2 %shard_map.105 = (bf16[64,6144]{1,0:T(8,128)(2,1)}, bf16[48,64,128]{2,1,0:T(8,128)(2,1)}, f32[64,256]{1,0:T(8,128)}) custom-call(bf16[256,256]{1,0:T(8,128)(2,1)} %pad_maximum_fusion.weight, bf16[48,64,128]{2,1,0:T(8,128)(2,1)} %shard_map.104.a0, bf16[48,64,128]{2,1,0:T(8,128)(2,1)} %copy-done.5, bf16[48,64,128]{2,1,0:T(8,128)(2,1)} %copy-done.2, ...), custom_call_target="tpu_custom_call" | custom-call | flops 1207959552 | bytes 7864320 | tf_op jit(solution)/shard_map/pallas_call | solution.py:181
  236.3 10.0 %shard_map.106 = bf16[512,64,128]{2,1,0:T(8,128)(2,1)} custom-call(s32[256]{0:T(256)} %get-tuple-element.21.dest, s32[256]{0:T(256)} %pad_add_fusion.2.target, s32[256]{0:T(256)} %convert_element_type.46.again, s32[4]{0:T(128)} %pad_add_fusion.3.live, bf16[48,64,128]{2,1,0:T(8,128)(2,1)} %get-tuple-element.7.grads, bf16[64,128,128]{2,1,0:T(8,128)(2,1)} %bitcast.50, ...), custom_call_target="tpu_custom_call" | custom-call | flops 536870912 | bytes 16777216 | tf_op jit(solution)/shard_map/pallas_call | solution.py:236
  246.3 13.0 %all-to-all-start.2 = ((bf16[32,1024,128]{2,1,0:T(8,128)(2,1)}), bf16[32,1024,128]{2,1,0:T(8,128)(2,1)}, u32[]{:S(2)}, u32[]{:S(2)}) async-start(bf16[32,1024,128]{2,1,0:T(8,128)(2,1)} %bitcast.48), calls=%async_computation.2 | async-start | bytes 16777216 | tf_op jit(solution)/shard_map/all_to_all | solution.py:306
  259.6 1.8 collective-permute-start.15
  261.4 80.0 %collective-permute-done.15 = f32[64,256]{1,0:T(8,128)S(1)} collective-permute-done((f32[64,256]{1,0:T(8,128)S(1)}, f32[64,256]{1,0:T(8,128)S(1)}, u32[]{:S(2)}, u32[]{:S(2)}) %collective-permute-start.15) | collective-permute-done | bytes 65568 | tf_op jit(solution)/shard_map/ppermute | solution.py:371
  341.4 18.7 %collective-permute-start.16 = (f32[64,256]{1,0:T(8,128)S(1)}, f32[64,256]{1,0:T(8,128)S(1)}, u32[]{:S(2)}, u32[]{:S(2)}) collective-permute-start(f32[64,256]{1,0:T(8,128)S(1)} %fusion.15), channel_id=1, source_target_pairs={{0,8},{4,12},{8,0},{12,4},{16,24},{20,28},{24,16},{28,20},{32,40},... | collective-permute-start | bytes 196616 | tf_op jit(solution)/shard_map/ppermute | solution.py:371
  360.1 10.3 %collective-permute-done.16 = f32[64,256]{1,0:T(8,128)S(1)} collective-permute-done((f32[64,256]{1,0:T(8,128)S(1)}, f32[64,256]{1,0:T(8,128)S(1)}, u32[]{:S(2)}, u32[]{:S(2)}) %collective-permute-start.16) | collective-permute-done | bytes 65568 | tf_op jit(solution)/shard_map/ppermute | solution.py:371
  370.6 8.6 %collective-permute-done.17 = f32[64,256]{1,0:T(8,128)S(1)} collective-permute-done((f32[64,256]{1,0:T(8,128)S(1)}, f32[64,256]{1,0:T(8,128)S(1)}, u32[]{:S(2)}, u32[]{:S(2)}) %collective-permute-start.17) | collective-permute-done | bytes 65568 | tf_op jit(solution)/shard_map/ppermute | solution.py:371
  379.3 13.7 %collective-permute-start.18 = (f32[64,256]{1,0:T(8,128)S(1)}, f32[64,256]{1,0:T(8,128)S(1)}, u32[]{:S(2)}, u32[]{:S(2)}) collective-permute-start(f32[64,256]{1,0:T(8,128)S(1)} %add.33), channel_id=1, source_target_pairs={{0,32},{4,36},{8,40},{12,44},{16,48},{20,52},{24,56},{28,60},{32,0... | collective-permute-start | bytes 196616 | tf_op jit(solution)/shard_map/ppermute | solution.py:371
  393.1 2.1 collective-permute-done.18
  395.2 2.3 collective-permute-start.19
  397.5 0.6 broadcast_select_fusion.12.index
  398.1 3.0 collective-permute-done.19
  401.1 0.6 add_multiply_fusion
  401.7 18.1 %shard_map.107 = bf16[64,6144]{1,0:T(8,128)(2,1)} custom-call(s32[512]{0:T(512)} %broadcast_select_fusion.12.index, s32[32]{0:T(128)} %copy-done.10, bf16[32,1024,128]{2,1,0:T(8,128)(2,1)} %all-to-all-done.2.incoming), custom_call_target="tpu_custom_call" | custom-call | flops 4194304 | bytes 8388608 | tf_op jit(solution)/shard_map/pallas_call | solution.py:286
  (67 shorter events, 2.5 us)
Async XLA Ops:
  2.0 3.6 collective-permute-start.4
  4.1 1.8 collective-permute-start.3
  5.6 1.1 collective-permute-start.5
  43.2 5.2 %copy-start = (bf16[1,64,128,128]{3,2,1,0:T(8,128)(2,1)S(1)}, bf16[1,64,128,128]{3,2,1,0:T(8,128)(2,1)}, u32[]{:S(2)}) copy-start(bf16[1,64,128,128]{3,2,1,0:T(8,128)(2,1)} %param.11) | copy-start | bytes 6291460
  43.2 141.0 %copy-start.1 = (bf16[64,6144]{1,0:T(8,128)(2,1)S(1)}, bf16[64,6144]{1,0:T(8,128)(2,1)}, u32[]{:S(2)}) copy-start(bf16[64,6144]{1,0:T(8,128)(2,1)} %c0.1) | copy-start | bytes 2359300
  43.2 142.0 %copy-start.11 = (s32[1,64]{1,0:T(1,128)S(1)}, s32[1,64]{1,0:T(1,128)}, u32[]{:S(2)}) copy-start(s32[1,64]{1,0:T(1,128)} %param.12) | copy-start | bytes 772
  43.2 148.8 %all-to-all-start.1 = ((bf16[32,1024,128]{2,1,0:T(8,128)(2,1)}), bf16[32,1024,128]{2,1,0:T(8,128)(2,1)}, u32[]{:S(2)}, u32[]{:S(2)}) async-start(bf16[32,1024,128]{2,1,0:T(8,128)(2,1)} %shard_map.103), calls=%async_computation.1 | async-start | bytes 16777216 | tf_op jit(solution)/shard_map/all_to_all | solution.py:306
  48.5 135.7 %collective-permute-start.7 = (bf16[64,128,128]{2,1,0:T(8,128)(2,1)S(1)}, bf16[64,128,128]{2,1,0:T(8,128)(2,1)}, u32[]{:S(2)}, u32[]{:S(2)}) collective-permute-start(bf16[64,128,128]{2,1,0:T(8,128)(2,1)S(1)} %bitcast.51), channel_id=1, source_target_pairs={{0,2},{2,0},{1,3},{3,1},{4,6},{6,4},{5,7},{7,5},{8,10},{10,8},{9,1... | collective-permute-start | bytes 6291464 | tf_op jit(solution)/shard_map/ppermute | solution.py:27
  49.6 142.5 %collective-permute-start.6 = (bf16[64,128,128]{2,1,0:T(8,128)(2,1)S(1)}, bf16[64,128,128]{2,1,0:T(8,128)(2,1)}, u32[]{:S(2)}, u32[]{:S(2)}) collective-permute-start(bf16[64,128,128]{2,1,0:T(8,128)(2,1)S(1)} %bitcast.52), channel_id=1, source_target_pairs={{0,1},{1,0},{2,3},{3,2},{4,5},{5,4},{6,7},{7,6},{8,9},{9,8},{10,11... | collective-permute-start | bytes 6291464 | tf_op jit(solution)/shard_map/ppermute | solution.py:23
  184.2 7.8 %collective-permute-start.8 = (bf16[64,128,128]{2,1,0:T(8,128)(2,1)}, bf16[64,128,128]{2,1,0:T(8,128)(2,1)}, u32[]{:S(2)}, u32[]{:S(2)}) collective-permute-start(bf16[64,128,128]{2,1,0:T(8,128)(2,1)} %collective-permute-done.7.refs_2_), channel_id=1, source_target_pairs={{0,1},{1,0},{2,3},{3,2},{4,5},{5,4},{6,7},{7,6},{8,9},{9,8},{10,11... | collective-permute-start | bytes 6291464 | tf_op jit(solution)/shard_map/ppermute | solution.py:23
  184.2 20.3 %collective-permute-start.13 = (bf16[64,6144]{1,0:T(8,128)(2,1)S(1)}, bf16[64,6144]{1,0:T(8,128)(2,1)}, u32[]{:S(2)}, u32[]{:S(2)}) collective-permute-start(bf16[64,6144]{1,0:T(8,128)(2,1)S(1)} %copy-done.1), channel_id=1, source_target_pairs={{0,2},{2,0},{1,3},{3,1},{4,6},{6,4},{5,7},{7,5},{8,10},{10,8},{9,1... | collective-permute-start | bytes 2359304 | tf_op jit(solution)/shard_map/ppermute | solution.py:27
  192.1 11.2 %copy-start.8 = (bf16[64,256]{1,0:T(8,128)(2,1)S(1)}, bf16[64,256]{1,0:T(8,128)(2,1)}, u32[]{:S(2)}) copy-start(bf16[64,256]{1,0:T(8,128)(2,1)} %param.9) | copy-start | bytes 98308
  202.2 20.3 %collective-permute-start.10 = (bf16[48,64,128]{2,1,0:T(8,128)(2,1)}, bf16[48,64,128]{2,1,0:T(8,128)(2,1)S(1)}, u32[]{:S(2)}, u32[]{:S(2)}) collective-permute-start(bf16[48,64,128]{2,1,0:T(8,128)(2,1)} %shard_map.104.a0), channel_id=1, source_target_pairs={{0,2},{2,0},{1,3},{3,1},{4,6},{6,4},{5,7},{7,5},{8,10},{10,8},{9,1... | collective-permute-start | bytes 2359304 | tf_op jit(solution)/shard_map/ppermute | solution.py:27
  203.3 1.5 collective-permute-start
  203.5 19.8 %collective-permute-start.1 = (bf16[64,256]{1,0:T(8,128)(2,1)S(1)}, bf16[64,256]{1,0:T(8,128)(2,1)S(1)}, u32[]{:S(2)}, u32[]{:S(2)}) collective-permute-start(bf16[64,256]{1,0:T(8,128)(2,1)S(1)} %copy-done.8), channel_id=1, source_target_pairs={{0,2},{2,0},{1,3},{3,1},{4,6},{6,4},{5,7},{7,5},{8,10},{10,8},{9,1... | collective-permute-start | bytes 98312 | tf_op jit(solution)/shard_map/ppermute | solution.py:27
  204.3 21.4 %collective-permute-start.12 = (bf16[64,6144]{1,0:T(8,128)(2,1)S(1)}, bf16[64,6144]{1,0:T(8,128)(2,1)S(1)}, u32[]{:S(2)}, u32[]{:S(2)}) collective-permute-start(bf16[64,6144]{1,0:T(8,128)(2,1)S(1)} %copy-done.1), channel_id=1, source_target_pairs={{0,1},{1,0},{2,3},{3,2},{4,5},{5,4},{6,7},{7,6},{8,9},{9,8},{10,11... | collective-permute-start | bytes 2359304 | tf_op jit(solution)/shard_map/ppermute | solution.py:23
  204.5 21.2 %collective-permute-start.14 = (bf16[64,6144]{1,0:T(8,128)(2,1)}, bf16[64,6144]{1,0:T(8,128)(2,1)S(1)}, u32[]{:S(2)}, u32[]{:S(2)}) collective-permute-start(bf16[64,6144]{1,0:T(8,128)(2,1)} %collective-permute-done.13.c2), channel_id=1, source_target_pairs={{0,1},{1,0},{2,3},{3,2},{4,5},{5,4},{6,7},{7,6},{8,9},{9,8},{10,11... | collective-permute-start | bytes 2359304 | tf_op jit(solution)/shard_map/ppermute | solution.py:23
  204.8 20.9 %collective-permute-start.9 = (bf16[48,64,128]{2,1,0:T(8,128)(2,1)}, bf16[48,64,128]{2,1,0:T(8,128)(2,1)S(1)}, u32[]{:S(2)}, u32[]{:S(2)}) collective-permute-start(bf16[48,64,128]{2,1,0:T(8,128)(2,1)} %shard_map.104.a0), channel_id=1, source_target_pairs={{0,1},{1,0},{2,3},{3,2},{4,5},{5,4},{6,7},{7,6},{8,9},{9,8},{10,11... | collective-permute-start | bytes 2359304 | tf_op jit(solution)/shard_map/ppermute | solution.py:23
  222.5 3.3 copy-start.2
  222.5 3.3 collective-permute-start.11
  223.3 1.5 collective-permute-start.2
  225.7 0.9 copy-start.3
  225.8 1.2 copy-start.4
  225.8 1.4 copy-start.5
  227.2 0.9 copy-start.6
  246.3 13.1 %copy-start.7 = (f32[64,256]{1,0:T(8,128)S(1)}, f32[64,256]{1,0:T(8,128)}, u32[]{:S(2)}) copy-start(f32[64,256]{1,0:T(8,128)} %get-tuple-element.8) | copy-start | bytes 196612
  246.3 151.2 %copy-start.9 = (s32[512]{0:T(512)S(1)}, s32[512]{0:T(512)}, u32[]{:S(2)}) copy-start(s32[512]{0:T(512)} %reshape.160.index) | copy-start | bytes 6148
  246.3 155.4 %all-to-all-start.2 = ((bf16[32,1024,128]{2,1,0:T(8,128)(2,1)}), bf16[32,1024,128]{2,1,0:T(8,128)(2,1)}, u32[]{:S(2)}, u32[]{:S(2)}) async-start(bf16[32,1024,128]{2,1,0:T(8,128)(2,1)} %bitcast.48), calls=%async_computation.2 | async-start | bytes 16777216 | tf_op jit(solution)/shard_map/all_to_all | solution.py:306
  259.6 81.8 %collective-permute-start.15 = (f32[64,256]{1,0:T(8,128)S(1)}, f32[64,256]{1,0:T(8,128)S(1)}, u32[]{:S(2)}, u32[]{:S(2)}) collective-permute-start(f32[64,256]{1,0:T(8,128)S(1)} %pad_maximum_fusion.1), channel_id=1, source_target_pairs={{0,4},{4,0},{8,12},{12,8},{16,20},{20,16},{24,28},{28,24},{32,36},... | collective-permute-start | bytes 196616 | tf_op jit(solution)/shard_map/ppermute | solution.py:371
  341.4 29.0 %collective-permute-start.16 = (f32[64,256]{1,0:T(8,128)S(1)}, f32[64,256]{1,0:T(8,128)S(1)}, u32[]{:S(2)}, u32[]{:S(2)}) collective-permute-start(f32[64,256]{1,0:T(8,128)S(1)} %fusion.15), channel_id=1, source_target_pairs={{0,8},{4,12},{8,0},{12,4},{16,24},{20,28},{24,16},{28,20},{32,40},... | collective-permute-start | bytes 196616 | tf_op jit(solution)/shard_map/ppermute | solution.py:371
  370.4 8.9 %collective-permute-start.17 = (f32[64,256]{1,0:T(8,128)S(1)}, f32[64,256]{1,0:T(8,128)S(1)}, u32[]{:S(2)}, u32[]{:S(2)}) collective-permute-start(f32[64,256]{1,0:T(8,128)S(1)} %add.32), channel_id=1, source_target_pairs={{0,16},{4,20},{8,24},{12,28},{16,0},{20,4},{24,8},{28,12},{32,48},... | collective-permute-start | bytes 196616 | tf_op jit(solution)/shard_map/ppermute | solution.py:371
  370.6 31.1 %copy-start.10 = (s32[32]{0:T(128)}, s32[32]{0:T(128)S(1)}, u32[]{:S(2)}) copy-start(s32[32]{0:T(128)S(1)} %slice_reduce_fusion.count) | copy-start | bytes 388
  379.3 15.9 %collective-permute-start.18 = (f32[64,256]{1,0:T(8,128)S(1)}, f32[64,256]{1,0:T(8,128)S(1)}, u32[]{:S(2)}, u32[]{:S(2)}) collective-permute-start(f32[64,256]{1,0:T(8,128)S(1)} %add.33), channel_id=1, source_target_pairs={{0,32},{4,36},{8,40},{12,44},{16,48},{20,52},{24,56},{28,60},{32,0... | collective-permute-start | bytes 196616 | tf_op jit(solution)/shard_map/ppermute | solution.py:371
  395.2 5.8 %collective-permute-start.19 = (f32[64,256]{1,0:T(8,128)S(1)}, f32[64,256]{1,0:T(8,128)S(1)}, u32[]{:S(2)}, u32[]{:S(2)}) collective-permute-start(f32[64,256]{1,0:T(8,128)S(1)} %add.34), channel_id=1, source_target_pairs={{0,64},{4,68},{8,72},{12,76},{16,80},{20,84},{24,88},{28,92},{32,9... | collective-permute-start | bytes 196616 | tf_op jit(solution)/shard_map/ppermute | solution.py:371
